TPU v7x, 32 devices: a whole 2x2x4 slice. The times are simulated.
32 devices in a mesh: ctx: 16 (over z, y, x), head: 2 (over core).
Axes of the slice: x: 2, y: 2, z: 4, core: 2. Of those that a mesh axis runs over, the one named last changes fastest.
Arguments:
- queries: bfloat16 [8192, 4096], P('ctx', 'head'), may hold values from -6 to 6
- keys: bfloat16 [8192, 4096], P('ctx', 'head'), may hold values from -6 to 6
- values: bfloat16 [8192, 4096], P('ctx', 'head'), may hold values from -6 to 6
- doc_start: int32 [32], P('ctx'), may hold values from 0 to 256, as said below
- decay_rate: float32 [32], P('head'), may hold values from 3.6621094e-05 to 0.032552083
- gain: float32 [4096], P('head'), may hold values from 0.25 to 1.75
- plan_offset: int32 [16], replicated, may hold values from 0 to 1, as said below
Outputs:
- mixed: bfloat16 [12288, 4096], P('ctx', 'head')
Inputs may be any that keep to these rules, and one draw needn't show every extreme that they name: `doc_start`: at most one document begins in a block. plan_offset[0] is 0 and every other entry is 0 or 1; some shard takes 2 * 2 - 1 blocks.
All inputs are finite; a program needn't handle non-finite values.
Results may differ from a plain program's by a relative error of at most 0.0011.
The roundings to bfloat16 on the way count: a program that leaves them out, or rounds other values in their place, can miss the bound.
Values may be sent and summed in bfloat16 or wider, within the bound.
A program may use at most 128 MiB of HBM per device.

v0:
```python
import jax
import jax.numpy as jnp
from jax import lax
from jax.sharding import PartitionSpec as P

HD = 128
BLOCK = 256


EPSILON = 1e-06


def carried_in(value, axis, combine, identity):
    devices, place = (lax.axis_size(axis), lax.axis_index(axis))
    everything = jax.tree.map(lambda part: lax.all_gather(part, axis), value)
    start = jax.tree.map(
        lambda part, zero: jnp.broadcast_to(jnp.asarray(zero, part.dtype), part.shape),
        value,
        identity,
    )

    def turn(k, before):
        reached = k < place
        new = combine(before, jax.tree.map(lambda part: part[k], everything))
        return jax.tree.map(lambda a, b: jnp.where(reached, a, b), new, before)

    return lax.fori_loop(0, devices, turn, start)


def passed_along(block, axis, distance):
    devices = range(lax.axis_size(axis))
    route = [(i - distance, i) for i in devices if i - distance in devices]
    return lax.ppermute(block, axis, route)


def attend(queries, keys, values, starts, active, rates, gain):
    row_count = queries.shape[0]
    columns = queries.shape[1]
    heads_here = columns // HD
    block_count = row_count // BLOCK
    shaped = (block_count, BLOCK, heads_here, HD)
    q_blocks = queries.reshape(shaped)
    k_blocks = keys.reshape(shaped)
    v_blocks = values.reshape(shaped)
    position = jnp.arange(BLOCK, dtype=jnp.int32)
    place_float = position.astype(jnp.float32)
    distance = place_float[:, None] - place_float[None, :]
    weights = jnp.where(
        distance[None] >= 0, jnp.exp(-rates[:, None, None] * jnp.maximum(distance, 0.0)[None]), 0.0
    )
    marks = starts[:, None, None]
    allowed = jnp.logical_not(
        (position[None, None, :] < marks) & (marks <= position[None, :, None])
    ).astype(jnp.float32)
    scores = jnp.einsum("bihd,bjhd->bhij", q_blocks, k_blocks, preferred_element_type=jnp.float32)
    probs = (scores * weights[None] * allowed[:, None]).astype(jnp.bfloat16)
    intra = jnp.einsum("bhij,bjhd->bihd", probs, v_blocks, preferred_element_type=jnp.float32)
    key_keep = (position[None, :] >= starts[:, None]).astype(jnp.float32)
    key_decay = jnp.exp(-rates[None, :] * (BLOCK - 1 - place_float)[:, None])
    weighted = (
        k_blocks.astype(jnp.float32) * key_decay[None, :, :, None] * key_keep[:, :, None, None]
    ).astype(jnp.bfloat16)
    updates = jnp.einsum("bjhd,bjhe->bhde", weighted, v_blocks, preferred_element_type=jnp.float32)
    carry = jnp.where((starts == BLOCK)[:, None], jnp.exp(-rates * BLOCK)[None, :], 0.0)
    carry = jnp.where(active[:, None], carry, 1.0)

    def compose(totals, pair_in):
        decay_now, update_now = pair_in
        return ((totals[0] * decay_now, decay_now[:, None, None] * totals[1] + update_now), None)

    identity = (jnp.ones((heads_here,), jnp.float32), jnp.zeros((heads_here, HD, HD), jnp.float32))
    (shard_decay, shard_state), _ = lax.scan(compose, identity, (carry, updates))

    def combine(earlier, later):
        return (earlier[0] * later[0], later[0][:, None, None] * earlier[1] + later[1])

    _, incoming = carried_in((shard_decay, shard_state), "ctx", combine, identity)

    def advance(state_now, pair_in):
        decay_now, update_now = pair_in
        return (decay_now[:, None, None] * state_now + update_now, state_now)

    _, states = lax.scan(advance, incoming, (carry, updates))
    query_decay = jnp.exp(-rates[None, :] * (place_float + 1.0)[:, None])
    query_keep = (position[None, :] < starts[:, None]).astype(jnp.float32)
    inter = jnp.einsum(
        "bihd,bhde->bihe", q_blocks.astype(jnp.float32), states, precision=lax.Precision.HIGHEST
    )
    attended = intra + inter * query_decay[None, :, :, None] * query_keep[:, :, None, None]
    attended = attended.reshape(row_count, columns)
    squares = jnp.sum(attended * attended, axis=1)
    totals = lax.psum(squares, "head")
    scaling = lax.rsqrt(totals / (columns * lax.axis_size("head")) + EPSILON)
    return (attended * scaling[:, None] * gain[None, :]).astype(jnp.bfloat16)


def body(queries, keys, values, doc_start, decay_rate, gain, plan_offset):
    blocks_here = doc_start.shape[0]
    slots = 2 * blocks_here - 1
    index = lax.axis_index("ctx")
    places = jnp.arange(plan_offset.shape[0], dtype=jnp.int32)
    offset_here = jnp.sum(jnp.where(places == index, plan_offset, 0))
    offset_next = jnp.sum(jnp.where(places == index + 1, plan_offset, 0))
    length = blocks_here + offset_next - offset_here
    active = jnp.arange(slots, dtype=jnp.int32) < length
    active_rows = jnp.repeat(active, BLOCK)

    def window_rows(local_rows, next_rows):
        padding_rows = jnp.zeros(((blocks_here - 1) * BLOCK, local_rows.shape[1]), local_rows.dtype)
        joined = jnp.concatenate([local_rows, next_rows, padding_rows], axis=0)
        picked = lax.dynamic_slice_in_dim(joined, offset_here * BLOCK, slots * BLOCK, 0)
        return jnp.where(active_rows[:, None], picked, jnp.zeros((), local_rows.dtype))

    following = passed_along((queries, keys, values, doc_start), "ctx", -1)
    q_window = window_rows(queries, following[0])
    k_window = window_rows(keys, following[1])
    v_window = window_rows(values, following[2])
    padding_marks = jnp.full((blocks_here - 1,), BLOCK, jnp.int32)
    joined_marks = jnp.concatenate([doc_start, following[3], padding_marks], axis=0)
    picked_marks = lax.dynamic_slice_in_dim(joined_marks, offset_here, slots, 0)
    starts = jnp.where(active, picked_marks, BLOCK)
    return attend(q_window, k_window, v_window, starts, active, decay_rate, gain)


def solution(mesh):
    in_specs = (
        P("ctx", "head"),
        P("ctx", "head"),
        P("ctx", "head"),
        P("ctx"),
        P("head"),
        P("head"),
        P(),
    )
    out_specs = P("ctx", "head")
    return jax.shard_map(body, mesh=mesh, in_specs=in_specs, out_specs=out_specs, check_vma=False)
```

profile of v0, /device:TPU:23, one launch (start us, length us, event | category | flops | bytes accessed | tf_op | source)
XLA Modules:
  0.0 434.7 jit_solution(8532931092502603955)
XLA Ops:
  6.5 2.2 collective-permute-start
  8.7 3.1 collective-permute-start.1
  11.8 2.2 collective-permute-start.2
  13.9 4.0 collective-permute-start.3
  17.9 1.3 fusion.38
  23.0 0.1 pad_dynamic-slice_fusion.6
  23.1 0.7 multiply_exponential_fusion.2
  23.8 0.1 multiply_exponential_fusion.1
  23.9 123.1 %collective-permute-done.3 = s32[2]{0:T(128)S(1)} collective-permute-done((s32[2]{0:T(128)}, s32[2]{0:T(128)S(1)}, u32[]{:S(2)}, u32[]{:S(2)}) %collective-permute-start.3) | collective-permute-done | bytes 40 | tf_op jit(solution)/shard_map/ppermute | solution.py:33
  146.9 0.7 pad_add_fusion
  147.6 0.1 broadcast_compare_fusion
  147.7 0.1 broadcast_in_dim.118
  147.8 0.1 select_select_fusion
  147.9 0.1 fusion.35
  148.0 9.7 %fusion.19 = (bf16[96,8,16,128]{3,1,2,0:T(8,128)(2,1)}, bf16[96,8,16,128]{3,1,2,0:T(8,128)(2,1)}, bf16[96,8,16,128]{3,1,2,0:T(8,128)(2,1)S(1)}) fusion(s32[]{:T(128)S(6)} %select_n.69, bf16[512,2048]{1,0:T(8,128)(2,1)} %param.13, bf16[512,2048]{1,0:T(8,128)(2,1)} %collective-permute-done.1, pred[768]{0:T(1024)(128)(4,1)S(1)} %broadcast_in_dim.119, ...), kind=kLoop, calls=%fused_computation.39 | loop fusion | flops 29884416 | bytes 22022404
  157.7 2.7 copy.30
  160.4 5.0 %copy.22 = bf16[3,256,16,128]{1,3,2,0:T(8,128)(2,1)} copy(bf16[3,256,16,128]{3,2,1,0:T(8,128)(2,1)} %bitcast.66) | data formatting | bytes 6291456 | tf_op jit(solution)/shard_map/reshape | solution.py:43
  165.4 3.0 copy.28
  168.5 3.3 fusion.24
  171.7 4.4 %while.40 = (s32[]{:T(128)}, f32[16]{0:T(128)S(1)}, f32[16,128,128]{2,1,0:T(8,128)S(1)}, f32[3,16]{1,0:T(4,128)S(1)}, f32[3,16,128,128]{3,2,1,0:T(8,128)}, /*index=5*/s32[]{:T(128)}, s32[]{:T(128)}) while((s32[]{:T(128)}, f32[16]{0:T(128)S(1)}, f32[16,128,128]{2,1,0:T(8,128)S(1)}, f32[3,16]{1,0:T(4,128)S(1)}, ...), condition=%wide.region_3.4_spmd.clone, body=%wide.region_2.3_spmd.clone.sunk | while | flops 786467 | bytes 3146144 | solution.py:72
  171.7 1.4 bitcast_add_fusion.6
  173.2 1.4 bitcast_add_fusion.6
  174.6 1.4 bitcast_add_fusion.6
  176.1 1.0 copy-done
  177.1 0.0 all-gather.4.cloned.1.call-update
  177.2 0.6 dynamic-slice
  178.7 0.1 subtract_compare_fusion
  178.9 0.1 subtract_maximum_fusion
  179.0 2.6 exponential_select_fusion
  181.6 0.2 not_convert_fusion
  181.8 2.7 copy.29
  184.5 0.2 dynamic-update-slice
  184.7 23.4 %all-reduce = f32[256]{0:T(256)S(1)} all-reduce(f32[256]{0:T(256)S(1)} %dynamic-update-slice), channel_id=2, replica_groups=mesh['ctx'=16,'head'=2] {'ctx'}, use_global_device_ids=true, to_apply=%add | all-reduce | flops 256 | bytes 2048
  208.1 0.1 reshape.257
  208.2 11.8 %fusion.3 = f32[3,16,128,256]{3,2,1,0:T(8,128)} fusion(f32[3,256,256]{2,1,0:T(8,128)S(1)} %not_convert_fusion, f32[16,256,256]{2,1,0:T(8,128)} %exponential_select_fusion, bf16[3,256,16,128]{1,3,2,0:T(8,128)(2,1)} %copy.22, bf16[3,256,16,128]{3,2,1,0:T(8,128)(2,1)} %bitcast.65, bf16[3,256,16,128]{3,2,1,0:T(8,128)(2,1)} %bitcast.61), kind=kOutput, calls=%fused_computation.13 | convolution fusion | flops 1620049920 | bytes 20709376 | tf_op jit(solution)/shard_map/bhij,bjhd->bihd/dot_general | solution.py:57
  220.0 148.1 %all-gather.4.cloned.1.call-done = f32[256,128,128]{2,1,0:T(8,128)} async-done(((f32[16,128,128]{2,1,0:T(8,128)}), f32[256,128,128]{2,1,0:T(8,128)}) %all-gather.4.cloned.1.call-update) | async-done | bytes 16777232 | tf_op jit(solution)/shard_map/all_gather | solution.py:15
  368.1 23.9 %while.41 = (s32[]{:T(128)}, f32[16,128,128]{2,1,0:T(8,128)S(1)}, s32[]{:T(128)}, f32[16,16]{1,0:T(8,128)S(1)}, f32[16,16,128,128]{3,2,1,0:T(8,128)}, /*index=5*/s32[]{:T(128)}, s32[]{:T(128)}) while((s32[]{:T(128)}, f32[16,128,128]{2,1,0:T(8,128)S(1)}, s32[]{:T(128)}, f32[16,16]{1,0:T(8,128)S(1)}, f32[16,16,128,128]{3,2,1,0:T(8,128)}, ...), condition=%wide.region_5.6_spmd.clone, body=%wide.region_4.5_spmd.clone.sunk | while | flops 1048580 | bytes 3146025 | solution.py:27
  368.1 1.5 fusion.48
  369.6 1.5 fusion.48
  371.1 1.5 fusion.48
  372.6 1.5 fusion.48
  374.1 1.5 fusion.48
  375.6 1.5 fusion.48
  377.1 1.5 fusion.48
  378.6 1.5 fusion.48
  380.1 1.5 fusion.48
  381.6 1.5 fusion.48
  383.1 1.5 fusion.48
  384.6 1.5 fusion.48
  386.1 1.5 fusion.48
  387.6 1.5 fusion.48
  389.1 1.5 fusion.48
  390.6 1.5 fusion.48
  392.0 7.6 %while.39 = (s32[]{:T(128)}, f32[16,128,128]{2,1,0:T(8,128)S(1)}, f32[3,16,128,128]{3,2,1,0:T(8,128)}, f32[3,16]{1,0:T(4,128)S(1)}, f32[3,16,128,128]{3,2,1,0:T(8,128)}, /*index=5*/s32[]{:T(128)}) while((s32[]{:T(128)}, f32[16,128,128]{2,1,0:T(8,128)S(1)}, f32[3,16,128,128]{3,2,1,0:T(8,128)}, f32[3,16]{1,0:T(4,128)S(1)}, ...), condition=%wide.region_7.8_spmd, body=%wide.region_6.7_spmd.sunk | while | flops 524290 | bytes 5243661 | solution.py:83
  392.0 1.1 bitcast_dynamic-update-slice_fusion.2
  393.1 1.4 bitcast_add_fusion.5
  394.6 1.1 bitcast_dynamic-update-slice_fusion.2
  395.6 1.4 bitcast_add_fusion.5
  397.1 1.1 bitcast_dynamic-update-slice_fusion.2
  398.2 1.4 bitcast_add_fusion.5
  399.6 11.1 %multiply_reduce_fusion = (f32[3,256]{1,0:T(4,128)S(1)}, f32[3,256,16,128]{1,3,2,0:T(8,128)}) fusion(f32[3,256]{1,0:T(4,128)S(1)} %get-tuple-element.237, f32[256,16]{0,1:T(8,128)S(1)} %get-tuple-element.234, f32[3,16,128,128]{3,2,1,0:T(8,128)} %get-tuple-element.157, bf16[3,256,16,128]{3,2,1,0:T(8,128)(2,1)} %bitcast.62, f32[3,16,128,256]{3,2,1,0:T(8,128)} %fusion.3), kind=kOutput, calls=%fused_computation.20 | convolution fusion | flops 2423782656 | bytes 18896896 | tf_op jit(solution)/shard_map/bihd,bhde->bihe/dot_general | solution.py:86
  410.7 6.7 %copy.26 = f32[3,256,16,128]{3,2,1,0:T(8,128)} copy(f32[3,256,16,128]{1,3,2,0:T(8,128)} %get-tuple-element.242) | data formatting | bytes 12582912 | tf_op jit(solution)/shard_map/add | solution.py:89
  417.4 3.2 psum.7
  420.5 7.3 %fusion.5 = bf16[768,2048]{1,0:T(8,128)(2,1)} fusion(f32[96,8,16,128]{3,2,1,0:T(8,128)} %bitcast.63, f32[2048]{0:T(1024)S(1)} %copy-done.4, f32[768]{0:T(1024)S(1)} %add_rsqrt_fusion), kind=kLoop, calls=%fused_computation.16 | loop fusion | flops 4718592 | bytes 9448448 | tf_op jit(solution)/shard_map/convert_element_type | solution.py:94
  (48 shorter events, 0.3 us)
Async XLA Ops:
  6.5 361.5 %all-gather.4.cloned.1.call-start = ((), (), s32[]{:S(2)}) async-start(), calls=%async_computation | async-start | bytes 17825792 | tf_op jit(solution)/shard_map/all_gather | solution.py:15
  6.5 141.4 %collective-permute-start = (bf16[512,2048]{1,0:T(8,128)(2,1)}, bf16[512,2048]{1,0:T(8,128)(2,1)S(1)}, u32[]{:S(2)}, u32[]{:S(2)}) collective-permute-start(bf16[512,2048]{1,0:T(8,128)(2,1)} %param.15), channel_id=1, source_target_pairs={{2,0},{4,2},{6,4},{8,6},{10,8},{12,10},{14,12},{16,14},{18,16},{20... | collective-permute-start | bytes 6291464 | tf_op jit(solution)/shard_map/ppermute | solution.py:33
  8.7 139.3 %collective-permute-start.1 = (bf16[512,2048]{1,0:T(8,128)(2,1)}, bf16[512,2048]{1,0:T(8,128)(2,1)}, u32[]{:S(2)}, u32[]{:S(2)}) collective-permute-start(bf16[512,2048]{1,0:T(8,128)(2,1)} %param.13), channel_id=1, source_target_pairs={{2,0},{4,2},{6,4},{8,6},{10,8},{12,10},{14,12},{16,14},{18,16},{20... | collective-permute-start | bytes 6291464 | tf_op jit(solution)/shard_map/ppermute | solution.py:33
  11.8 136.2 %collective-permute-start.2 = (bf16[512,2048]{1,0:T(8,128)(2,1)}, bf16[512,2048]{1,0:T(8,128)(2,1)}, u32[]{:S(2)}, u32[]{:S(2)}) collective-permute-start(bf16[512,2048]{1,0:T(8,128)(2,1)} %param.14), channel_id=1, source_target_pairs={{2,0},{4,2},{6,4},{8,6},{10,8},{12,10},{14,12},{16,14},{18,16},{20... | collective-permute-start | bytes 6291464 | tf_op jit(solution)/shard_map/ppermute | solution.py:33
  13.9 133.0 %collective-permute-start.3 = (s32[2]{0:T(128)}, s32[2]{0:T(128)S(1)}, u32[]{:S(2)}, u32[]{:S(2)}) collective-permute-start(s32[2]{0:T(128)} %param.16), channel_id=1, source_target_pairs={{2,0},{4,2},{6,4},{8,6},{10,8},{12,10},{14,12},{16,14},{18,16},{20... | collective-permute-start | bytes 32 | tf_op jit(solution)/shard_map/ppermute | solution.py:33
  165.4 3.1 copy-start.1
  168.4 3.3 copy-start.2
  171.7 5.4 %copy-start.5 = (u32[32]{0:T(128)S(1)}, u32[32]{0:T(128)}, u32[]{:S(2)}) copy-start(u32[32]{0:T(128)} %constant.86) | copy-start | bytes 388
  176.1 1.0 copy-start
  177.1 4.6 %copy-start.3 = (bf16[96,8,16,128]{3,1,2,0:T(8,128)(2,1)S(1)}, bf16[96,8,16,128]{3,1,2,0:T(8,128)(2,1)}, u32[]{:S(2)}) copy-start(bf16[96,8,16,128]{3,1,2,0:T(8,128)(2,1)} %get-tuple-element.230) | copy-start | bytes 9437188
  410.7 9.9 %copy-start.4 = (f32[2048]{0:T(1024)S(1)}, f32[2048]{0:T(1024)}, u32[]{:S(2)}) copy-start(f32[2048]{0:T(1024)} %param.18) | copy-start | bytes 24580
Sparse Core Ops, SparseCore 0:
  177.2 190.8 all-gather.3
where the time goes:
time: 439 us; the launch traced here: 435 us
  waiting for transfers between devices  271 us (62%)
  other arithmetic  55 us (13%)
  blocking collectives  26.6 us (6%)
  matrix products  26.1 us (6%)
  local copies, waits for them, and re-layouts  25.5 us (6%)
  between operations  18.3 us (4%)
  starting transfers between devices  11.3 us (3%)
    all_gather x1, waiting for transfers between devices, carried_in(): everything = jax.tree.map(lambda part: lax.all_gather(part, axis), value)  148 us
    ppermute x4, waiting for transfers between devices, passed_along(): return lax.ppermute(block, axis, route)  123 us
    unnamed x1, blocking collectives  23.4 us
    select_n x16, other arithmetic, turn(): return jax.tree.map(lambda a, b: jnp.where(reached, a, b), new, before)  23.3 us
    dot_general x1, matrix products, attend(): jnp.einsum('bhij,bjhd->bihd', probs, v_blocks, preferred_element_type=jnp...  11.8 us
    ppermute x4, starting transfers between devices, passed_along(): return lax.ppermute(block, axis, route)  11.3 us
    dot_general x1, matrix products, attend(): jnp.einsum('bihd,bhde->bihe', q_blocks.astype(jnp.float32), states, preci...  11.1 us
    unnamed x18, local copies, waits for them, and re-layouts  10.3 us
  transfers between devices with their start and end apart: 5, of which 2 were waited for; matrix products, arithmetic and copies ran while one was open for 5% of the time, Pallas kernels for 0%

commit v1 on v0

v1 whole, which is shorter than its diff:
```python
import functools

import jax
import jax.numpy as jnp
from jax import lax
from jax.experimental import pallas as pl
from jax.experimental.pallas import tpu as pltpu
from jax.sharding import PartitionSpec as P

HD = 128
BLOCK = 256
GROUP = 4
EPSILON = 1e-06
F32 = jnp.float32
BF16 = jnp.bfloat16
CHUNKS = 4
CROWS = BLOCK // CHUNKS


def dot(a, b, dims):
    return lax.dot_general(a, b, (dims, ((), ())), preferred_element_type=F32)


def kernel(
    n, hn, heads, width,
    start_ref, rate_ref, plan_ref, q_ref, k_ref, v_ref, gain_ref,
    out_ref,
    att, u0, mask, dist, sbuf, p1, pre, chain_in, chain_out, p3out, p3,
    ssq, ssq_in, halo_out, own1, halo_in,
    p1_send, p1_recv, ch_send, ch_recv, p3_send, p3_recv, sq_send, sq_recv, ha_send, ha_recv,
):
    hq = heads // GROUP
    zs = n // GROUP
    p = lax.axis_index("ctx")
    me = lax.axis_index("head")
    g = p // GROUP
    r = p % GROUP
    base = g * GROUP

    barrier = pltpu.get_barrier_semaphore()

    def greet(ctx, head):
        pl.semaphore_signal(
            barrier, inc=1, device_id=(ctx, head), device_id_type=pl.DeviceIdType.MESH
        )

    for t in range(1, GROUP):
        greet(base + (r + t) % GROUP, me)
    for t in range(1, hn):
        greet(p, (me + t) % hn)
    pl.when(g > 0)(lambda: greet(p - GROUP, me))
    pl.when(g < zs - 1)(lambda: greet(p + GROUP, me))
    pl.when(p > 0)(lambda: greet(p - 1, me))
    pl.when(p < n - 1)(lambda: greet(p + 1, me))

    start = [start_ref[0], start_ref[1]]
    flag = [jnp.where(s == BLOCK, 1.0, 0.0).astype(F32) for s in start]

    def cols(h):
        return pl.ds(pl.multiple_of(h * HD, HD), HD)

    def rows(b):
        return pl.ds(b * BLOCK, BLOCK)

    def power(h, count):
        return jnp.exp(jnp.full((1, HD), -rate_ref[h] * count, F32))

    def remote(src, dst, send, recv, ctx, head):
        return pltpu.make_async_remote_copy(
            src_ref=src, dst_ref=dst, send_sem=send, recv_sem=recv,
            device_id=(ctx, head), device_id_type=pl.DeviceIdType.MESH,
        )

    place = lax.broadcasted_iota(jnp.int32, (BLOCK, HD), 0)
    place_f = place.astype(F32)

    def shard_state(h):
        decay = jnp.exp(-rate_ref[h] * (BLOCK - 1 - place_f))
        parts = []
        for b in range(2):
            keys = k_ref[rows(b), cols(h)].astype(F32) * decay
            weighted = jnp.where(place >= start[b], keys, 0.0).astype(BF16)
            parts.append(dot(weighted, v_ref[rows(b), cols(h)], ((0,), (0,))))
        u0[h] = parts[0]
        return (flag[1] * power(h, float(BLOCK))) * parts[0] + parts[1]

    both = jnp.full((8, HD), flag[0] * flag[1], F32)

    def p1_copy(c, t):
        to = (r + t) % GROUP
        return remote(sbuf.at[c, t - 1], p1.at[c, r], p1_send.at[c, t - 1], p1_recv.at[c, r], base + to, me)

    def p1_arrival(c, t):
        src = (r + t) % GROUP
        return remote(sbuf.at[c, t - 1], p1.at[c, src], p1_send.at[c, t - 1], p1_recv.at[c, src], base + src, me)

    def first(c, carry):
        for t in (1, 2, 3):
            to = (r + t) % GROUP
            sbuf[c, t - 1, 0:HD] = shard_state(to * hq + c)
            sbuf[c, t - 1, HD:HD + 8] = both
        p1[c, r, 0:HD] = shard_state(r * hq + c)
        p1[c, r, HD:HD + 8] = both

        @pl.when(c == 0)
        def _():
            expected = GROUP - 1 + hn - 1
            expected = expected + jnp.where(g > 0, 1, 0) + jnp.where(g < zs - 1, 1, 0)
            expected = expected + jnp.where(p > 0, 1, 0) + jnp.where(p < n - 1, 1, 0)
            pl.semaphore_wait(barrier, expected)

        for t in (1, 2, 3):
            p1_copy(c, t).start()
        return carry

    lax.fori_loop(0, hq, first, 0)

    i_at = lax.broadcasted_iota(jnp.int32, (BLOCK, BLOCK), 0)
    j_at = lax.broadcasted_iota(jnp.int32, (BLOCK, BLOCK), 1)
    apart = i_at - j_at
    dist[...] = jnp.maximum(apart, 0).astype(F32)
    for b in range(2):
        blocked = (j_at < start[b]) & (start[b] <= i_at)
        mask[b] = jnp.where(blocked, 0.0, jnp.where(apart >= 0, 1.0, 0.0))

    per = 2

    def intra(step, carry):
        for s in range(per):
            h = step * per + s
            weights = jnp.exp(-rate_ref[h] * dist[...])
            for b in range(2):
                scores = dot(q_ref[rows(b), cols(h)], k_ref[rows(b), cols(h)], ((1,), (1,)))
                probs = (scores * weights * mask[b]).astype(BF16)
                att[rows(b), cols(h)] = dot(probs, v_ref[rows(b), cols(h)], ((1,), (0,)))
        return carry

    lax.fori_loop(0, heads // per, intra, 0)

    def prefix(c, carry):
        h = r * hq + c
        for t in (1, 2, 3):
            p1_arrival(c, t).wait_recv()
        decay = power(h, 2.0 * BLOCK)
        total = jnp.zeros((HD, HD), F32)
        reach = jnp.ones((1, HD), F32)
        pre[c, 0, 0:HD] = total
        pre[c, 0, HD:HD + 8] = jnp.ones((8, HD), F32)
        for s in range(GROUP):
            step = p1[c, s, HD:HD + 1] * decay
            total = step * total + p1[c, s, 0:HD]
            reach = reach * step
            pre[c, s + 1, 0:HD] = total
            pre[c, s + 1, HD:HD + 8] = jnp.broadcast_to(reach, (8, HD))
        return carry

    lax.fori_loop(0, hq, prefix, 0)

    def ch_copy(c):
        return remote(chain_out.at[c], chain_in.at[c], ch_send.at[c], ch_recv.at[c], p + GROUP, me)

    def p3_copy(c, t):
        to = (r + t) % GROUP
        return remote(p3out.at[c, t - 1], p3.at[c, r], p3_send.at[c, t - 1], p3_recv.at[c, r], base + to, me)

    def p3_arrival(c, t):
        src = (r + t) % GROUP
        return remote(p3out.at[c, t - 1], p3.at[c, src], p3_send.at[c, t - 1], p3_recv.at[c, src], base + src, me)

    def onward(c, carry):
        @pl.when(g == 0)
        def _():
            chain_in[c] = jnp.zeros((HD, HD), F32)

        @pl.when(g > 0)
        def _():
            remote(chain_out.at[c], chain_in.at[c], ch_send.at[c], ch_recv.at[c], p - GROUP, me).wait_recv()

        @pl.when(g < zs - 1)
        def _():
            chain_out[c] = pre[c, GROUP, HD:HD + 1] * chain_in[c] + pre[c, GROUP, 0:HD]
            ch_copy(c).start()

        incoming = chain_in[c]
        for t in (1, 2, 3):
            to = (r + t) % GROUP
            p3out[c, t - 1] = pre[c, to, HD:HD + 1] * incoming + pre[c, to, 0:HD]
            p3_copy(c, t).start()
        p3[c, r] = pre[c, r, HD:HD + 1] * incoming + pre[c, r, 0:HD]
        return carry

    lax.fori_loop(0, hq, onward, 0)

    ssq[...] = jnp.zeros_like(ssq)

    def inter(c, carry):
        for t in range(GROUP):
            src = (r + t) % GROUP
            h = src * hq + c
            if t:
                p3_arrival(c, t).wait_recv()
            state = p3[c, src]
            decay = jnp.exp(-rate_ref[h] * (place_f + 1.0))
            for b in range(2):
                if b:
                    state = (flag[0] * power(h, float(BLOCK))) * state + u0[h]
                high = state.astype(BF16)
                low = (state - high.astype(F32)).astype(BF16)
                queries = q_ref[rows(b), cols(h)]
                got = dot(
                    jnp.concatenate([queries, queries], axis=1),
                    jnp.concatenate([high, low], axis=0),
                    ((1,), (0,)),
                )
                got = jnp.where(place < start[b], got * decay, 0.0)
                new = att[rows(b), cols(h)] + got
                att[rows(b), cols(h)] = new
                ssq[rows(b)] = ssq[rows(b)] + new * new
        return carry

    lax.fori_loop(0, hq, inter, 0)

    def sq_copy(t):
        return remote(ssq, ssq_in.at[t - 1], sq_send.at[t - 1], sq_recv.at[t - 1], p, (me + t) % hn)

    for t in range(1, hn):
        sq_copy(t).start()
    for t in range(1, hn):
        sq_copy(t).wait_recv()

    def normed(start_row):
        at = pl.ds(start_row, CROWS)
        squares = ssq[at]
        for t in range(1, hn):
            squares = squares + ssq_in[t - 1, at]
        totals = jnp.sum(squares, axis=1, keepdims=True)
        scaling = lax.rsqrt(totals / (width * hn) + EPSILON)
        return (att[at, :] * scaling * gain_ref[...]).astype(BF16)

    def part(i):
        return pl.ds(i * CROWS, CROWS)

    def ha_copy(i, ctx):
        return remote(halo_out.at[part(i)], halo_in.at[part(i)], ha_send.at[i], ha_recv.at[i], ctx, me)

    for i in range(CHUNKS):
        halo_out[part(i)] = normed(i * CROWS)

        @pl.when(p > 0)
        def _():
            ha_copy(i, p - 1).start()

    here = plan_ref[p]
    there = jnp.where(p < n - 1, plan_ref[jnp.minimum(p + 1, n - 1)], 0)

    for i in range(CHUNKS):
        own1[part(i)] = normed(BLOCK + i * CROWS)
        out_ref[part(i)] = jnp.where(here == 0, halo_out[part(i)], own1[part(i)])

    @pl.when(p == n - 1)
    def _():
        halo_in[...] = jnp.zeros_like(halo_in)

    for i in range(CHUNKS):
        @pl.when(p < n - 1)
        def _():
            ha_copy(i, p + 1).wait_recv()

        following = jnp.where(there == 1, halo_in[part(i)], jnp.zeros((), BF16))
        out_ref[pl.ds(BLOCK + i * CROWS, CROWS)] = jnp.where(here == 0, own1[part(i)], following)
        out_ref[pl.ds(2 * BLOCK + i * CROWS, CROWS)] = jnp.where(
            here == 0, following, jnp.zeros((), BF16)
        )

    def drain(c, carry):
        for t in (1, 2, 3):
            p1_copy(c, t).wait_send()
            p3_copy(c, t).wait_send()

        @pl.when(g < zs - 1)
        def _():
            ch_copy(c).wait_send()

        return carry

    lax.fori_loop(0, hq, drain, 0)
    for t in range(1, hn):
        sq_copy(t).wait_send()
    for i in range(CHUNKS):
        @pl.when(p > 0)
        def _():
            ha_copy(i, p - 1).wait_send()


def body(n, hn, queries, keys, values, doc_start, decay_rate, gain, plan_offset):
    width = queries.shape[1]
    heads = width // HD
    hq = heads // GROUP
    vmem = pl.BlockSpec(memory_space=pltpu.VMEM)
    smem = pl.BlockSpec(memory_space=pltpu.SMEM)
    dma = pltpu.SemaphoreType.DMA
    partners = max(hn - 1, 1)
    return pl.pallas_call(
        functools.partial(kernel, n, hn, heads, width),
        out_shape=jax.ShapeDtypeStruct((3 * BLOCK, width), BF16),
        in_specs=[smem, smem, smem, vmem, vmem, vmem, vmem],
        out_specs=vmem,
        scratch_shapes=[
            pltpu.VMEM((2 * BLOCK, width), F32),
            pltpu.VMEM((heads, HD, HD), F32),
            pltpu.VMEM((2, BLOCK, BLOCK), F32),
            pltpu.VMEM((BLOCK, BLOCK), F32),
            pltpu.VMEM((hq, GROUP - 1, HD + 8, HD), F32),
            pltpu.VMEM((hq, GROUP, HD + 8, HD), F32),
            pltpu.VMEM((hq, GROUP + 1, HD + 8, HD), F32),
            pltpu.VMEM((hq, HD, HD), F32),
            pltpu.VMEM((hq, HD, HD), F32),
            pltpu.VMEM((hq, GROUP - 1, HD, HD), F32),
            pltpu.VMEM((hq, GROUP, HD, HD), F32),
            pltpu.VMEM((2 * BLOCK, HD), F32),
            pltpu.VMEM((partners, 2 * BLOCK, HD), F32),
            pltpu.VMEM((BLOCK, width), BF16),
            pltpu.VMEM((BLOCK, width), BF16),
            pltpu.VMEM((BLOCK, width), BF16),
            dma((hq, GROUP - 1)),
            dma((hq, GROUP)),
            dma((hq,)),
            dma((hq,)),
            dma((hq, GROUP - 1)),
            dma((hq, GROUP)),
            dma((partners,)),
            dma((partners,)),
            dma((CHUNKS,)),
            dma((CHUNKS,)),
        ],
        compiler_params=pltpu.CompilerParams(
            collective_id=0, has_side_effects=True, vmem_limit_bytes=48 * 1024 * 1024
        ),
    )(doc_start, decay_rate, plan_offset, queries, keys, values, gain.reshape(1, width))


def solution(mesh):
    in_specs = (
        P("ctx", "head"),
        P("ctx", "head"),
        P("ctx", "head"),
        P("ctx"),
        P("head"),
        P("head"),
        P(),
    )
    return jax.shard_map(
        functools.partial(body, mesh.shape["ctx"], mesh.shape["head"]),
        mesh=mesh,
        in_specs=in_specs,
        out_specs=P("ctx", "head"),
        check_vma=False,
    )
```

time: 439 us -> 75.8 us (0.17)
  waiting for transfers between devices: 271 us -> 0 us
  Pallas kernels: 0 us -> 65.1 us
  other arithmetic: 55 us -> 0 us
  blocking collectives: 26.6 us -> 0 us
  matrix products: 26.1 us -> 0 us
  between operations: 18.3 us -> 0.02 us
  local copies, waits for them, and re-layouts: 25.5 us -> 9.81 us
  starting transfers between devices: 11.3 us -> 0 us
    all_gather x1 -> x0, waiting for transfers between devices: 148 us -> none  [carried_in(): everything = jax.tree.map(lambda part: lax.all_gather(part, axis), value)]
    ppermute x4 -> x0, waiting for transfers between devices: 123 us -> none  [passed_along(): return lax.ppermute(block, axis, route)]
    pallas_call x0 -> x1, Pallas kernels: none -> 65.1 us  [body(): pl.pallas_call(functools.partial(kernel, n, hn, heads, width), out_shape=...]
    dot_general x3 -> x0, matrix products: 26.1 us -> none  [the longest x1 11.8 us: attend(): jnp.einsum('bhij,bjhd->bihd', probs, v_blocks, preferred_element_type=jnp...]
    select_n x18 -> x0, other arithmetic: 26 us -> none  [the longest x16 23.3 us: turn(): return jax.tree.map(lambda a, b: jnp.where(reached, a, b), new, before)]
    unnamed x1 -> x0, blocking collectives: 23.4 us -> none
    ppermute x4 -> x0, starting transfers between devices: 11.3 us -> none  [passed_along(): return lax.ppermute(block, axis, route)]
    unnamed x4 -> x0, other arithmetic: 9.71 us -> none
  transfers between devices with their start and end apart: 5 -> 0, of which waited for: 2 -> 0; matrix products, arithmetic and copies ran while one was open for 5% -> 0% of each run, Pallas kernels for 0% -> 0%
where the time goes in v1:
time: 75.8 us; the launch traced here: 74.9 us
  Pallas kernels  65.1 us (86%)
  local copies, waits for them, and re-layouts  9.81 us (13%)
    pallas_call x1, Pallas kernels, body(): pl.pallas_call(functools.partial(kernel, n, hn, heads, width), out_shape=...  65.1 us
    unnamed x13, local copies, waits for them, and re-layouts  9.81 us

profile of v1, /device:TPU:23, one launch (start us, length us, event | category | flops | bytes accessed | tf_op | source)
XLA Modules:
  0.0 74.9 jit_solution(2457350850561692328)
XLA Ops:
  0.0 0.0 copy-start
  0.0 1.6 %copy-done = bf16[512,2048]{1,0:T(8,128)(2,1)S(1)} copy-done((bf16[512,2048]{1,0:T(8,128)(2,1)S(1)}, bf16[512,2048]{1,0:T(8,128)(2,1)}, u32[]{:S(2)}) %copy-start) | copy-done | bytes 2097176
  1.6 0.0 copy-start.1
  1.6 1.6 %copy-done.1 = bf16[512,2048]{1,0:T(8,128)(2,1)S(1)} copy-done((bf16[512,2048]{1,0:T(8,128)(2,1)S(1)}, bf16[512,2048]{1,0:T(8,128)(2,1)}, u32[]{:S(2)}) %copy-start.1) | copy-done | bytes 2097176
  3.2 0.0 copy-start.2
  3.2 0.7 copy-done.2
  3.9 0.0 copy-start.3
  3.9 0.7 copy-done.3
  4.5 0.0 copy-start.4
  4.5 0.7 copy-done.4
  5.2 0.0 copy-start.5
  5.2 0.7 copy-done.5
  5.8 65.1 %shard_map.73 = bf16[768,2048]{1,0:T(8,128)(2,1)} custom-call(s32[2]{0:T(128)S(1)} %copy-done.3, f32[16]{0:T(128)S(1)} %copy-done.4, s32[16]{0:T(128)S(1)} %copy-done.5, bf16[512,2048]{1,0:T(8,128)(2,1)S(1)} %copy-done, bf16[512,2048]{1,0:T(8,128)(2,1)S(1)} %copy-done.1, bf16[512,2048]{1,0:T(8,128)(2,1)} %v_ref.1, f32[1,2048]{1,0:T(1,128)S(1)} %bitcast.1), custom_call_target="tpu_custom_call" | custom-call | tf_op jit(solution)/shard_map/pallas_call | solution.py:303
  70.9 4.0 %copy.9 = bf16[768,2048]{1,0:T(8,128)(2,1)} copy(bf16[768,2048]{1,0:T(8,128)(2,1)} %shard_map.73) | data formatting | bytes 6291456
Async XLA Ops:
  0.0 1.6 %copy-start = (bf16[512,2048]{1,0:T(8,128)(2,1)S(1)}, bf16[512,2048]{1,0:T(8,128)(2,1)}, u32[]{:S(2)}) copy-start(bf16[512,2048]{1,0:T(8,128)(2,1)} %q_ref.1) | copy-start | bytes 6291460
  1.6 1.6 %copy-start.1 = (bf16[512,2048]{1,0:T(8,128)(2,1)S(1)}, bf16[512,2048]{1,0:T(8,128)(2,1)}, u32[]{:S(2)}) copy-start(bf16[512,2048]{1,0:T(8,128)(2,1)} %k_ref.1) | copy-start | bytes 6291460
  3.2 0.7 copy-start.2
  3.9 0.7 copy-start.3
  4.5 0.7 copy-start.4
  5.2 0.7 copy-start.5

commit v2 on v1

--- a/solution.py
+++ b/solution.py
@@ -23,11 +23,12 @@
 
 def kernel(
     n, hn, heads, width,
-    start_ref, rate_ref, plan_ref, q_ref, k_ref, v_ref, gain_ref,
+    start_ref, rate_ref, gain_ref, q_hbm, k_hbm, v_hbm,
     out_ref,
+    q_ref, k_ref, v_ref,
     att, u0, mask, dist, sbuf, p1, pre, chain_in, chain_out, p3out, p3,
-    ssq, ssq_in, halo_out, own1, halo_in,
-    p1_send, p1_recv, ch_send, ch_recv, p3_send, p3_recv, sq_send, sq_recv, ha_send, ha_recv,
+    ssq, ssq_in, own,
+    p1_send, p1_recv, ch_send, ch_recv, p3_send, p3_recv, sq_send, sq_recv, ha_send, ha_recv, in_sem, out_sem,
 ):
     hq = heads // GROUP
     zs = n // GROUP
@@ -36,6 +37,13 @@
     g = p // GROUP
     r = p % GROUP
     base = g * GROUP
+
+    loads = [
+        pltpu.make_async_copy(source, here, in_sem.at[i])
+        for i, (source, here) in enumerate(((k_hbm, k_ref), (v_hbm, v_ref), (q_hbm, q_ref)))
+    ]
+    for load in loads:
+        load.start()
 
     barrier = pltpu.get_barrier_semaphore()
 
@@ -113,6 +121,8 @@
             p1_copy(c, t).start()
         return carry
 
+    loads[0].wait()
+    loads[1].wait()
     lax.fori_loop(0, hq, first, 0)
 
     i_at = lax.broadcasted_iota(jnp.int32, (BLOCK, BLOCK), 0)
@@ -123,21 +133,16 @@
         blocked = (j_at < start[b]) & (start[b] <= i_at)
         mask[b] = jnp.where(blocked, 0.0, jnp.where(apart >= 0, 1.0, 0.0))
 
-    per = 2
-
-    def intra(step, carry):
-        for s in range(per):
-            h = step * per + s
+    def intra(step):
+        for s in range(GROUP):
+            h = step * GROUP + s
             weights = jnp.exp(-rate_ref[h] * dist[...])
             for b in range(2):
                 scores = dot(q_ref[rows(b), cols(h)], k_ref[rows(b), cols(h)], ((1,), (1,)))
                 probs = (scores * weights * mask[b]).astype(BF16)
                 att[rows(b), cols(h)] = dot(probs, v_ref[rows(b), cols(h)], ((1,), (0,)))
-        return carry
-
-    lax.fori_loop(0, heads // per, intra, 0)
-
-    def prefix(c, carry):
+
+    def prefix(c):
         h = r * hq + c
         for t in (1, 2, 3):
             p1_arrival(c, t).wait_recv()
@@ -152,9 +157,6 @@
             reach = reach * step
             pre[c, s + 1, 0:HD] = total
             pre[c, s + 1, HD:HD + 8] = jnp.broadcast_to(reach, (8, HD))
-        return carry
-
-    lax.fori_loop(0, hq, prefix, 0)
 
     def ch_copy(c):
         return remote(chain_out.at[c], chain_in.at[c], ch_send.at[c], ch_recv.at[c], p + GROUP, me)
@@ -168,6 +170,9 @@
         return remote(p3out.at[c, t - 1], p3.at[c, src], p3_send.at[c, t - 1], p3_recv.at[c, src], base + src, me)
 
     def onward(c, carry):
+        intra(c)
+        prefix(c)
+
         @pl.when(g == 0)
         def _():
             chain_in[c] = jnp.zeros((HD, HD), F32)
@@ -189,6 +194,7 @@
         p3[c, r] = pre[c, r, HD:HD + 1] * incoming + pre[c, r, 0:HD]
         return carry
 
+    loads[2].wait()
     lax.fori_loop(0, hq, onward, 0)
 
     ssq[...] = jnp.zeros_like(ssq)
@@ -241,36 +247,22 @@
         return pl.ds(i * CROWS, CROWS)
 
     def ha_copy(i, ctx):
-        return remote(halo_out.at[part(i)], halo_in.at[part(i)], ha_send.at[i], ha_recv.at[i], ctx, me)
-
-    for i in range(CHUNKS):
-        halo_out[part(i)] = normed(i * CROWS)
-
-        @pl.when(p > 0)
-        def _():
-            ha_copy(i, p - 1).start()
-
-    here = plan_ref[p]
-    there = jnp.where(p < n - 1, plan_ref[jnp.minimum(p + 1, n - 1)], 0)
-
-    for i in range(CHUNKS):
-        own1[part(i)] = normed(BLOCK + i * CROWS)
-        out_ref[part(i)] = jnp.where(here == 0, halo_out[part(i)], own1[part(i)])
-
-    @pl.when(p == n - 1)
-    def _():
-        halo_in[...] = jnp.zeros_like(halo_in)
-
-    for i in range(CHUNKS):
-        @pl.when(p < n - 1)
-        def _():
-            ha_copy(i, p + 1).wait_recv()
-
-        following = jnp.where(there == 1, halo_in[part(i)], jnp.zeros((), BF16))
-        out_ref[pl.ds(BLOCK + i * CROWS, CROWS)] = jnp.where(here == 0, own1[part(i)], following)
-        out_ref[pl.ds(2 * BLOCK + i * CROWS, CROWS)] = jnp.where(
-            here == 0, following, jnp.zeros((), BF16)
+        return remote(
+            own.at[part(i)], out_ref.at[pl.ds(2 * BLOCK + i * CROWS, CROWS)],
+            ha_send.at[i], ha_recv.at[i], ctx, me,
         )
+
+    def keep(i):
+        return pltpu.make_async_copy(own.at[part(i)], out_ref.at[part(i)], out_sem.at[i])
+
+    for i in range(2 * CHUNKS):
+        own[part(i)] = normed(i * CROWS)
+        if i < CHUNKS:
+            @pl.when(p > 0)
+            def _():
+                ha_copy(i, p - 1).start()
+
+        keep(i).start()
 
     def drain(c, carry):
         for t in (1, 2, 3):
@@ -286,10 +278,60 @@
     lax.fori_loop(0, hq, drain, 0)
     for t in range(1, hn):
         sq_copy(t).wait_send()
+    for i in range(2 * CHUNKS):
+        keep(i).wait()
     for i in range(CHUNKS):
         @pl.when(p > 0)
         def _():
             ha_copy(i, p - 1).wait_send()
+
+        @pl.when(p < n - 1)
+        def _():
+            ha_copy(i, p + 1).wait_recv()
+
+
+def placed(n, plan_ref, mine_ref, out_ref, slots, in_sem, out_sem):
+    p = lax.axis_index("ctx")
+    here = plan_ref[p]
+    there = jnp.where(p < n - 1, plan_ref[jnp.minimum(p + 1, n - 1)], 0)
+    length = 2 + there - here
+
+    def fetch(i):
+        row = pl.multiple_of(jnp.minimum(here + i, 2) * BLOCK, BLOCK)
+        return pltpu.make_async_copy(mine_ref.at[pl.ds(row, BLOCK)], slots.at[i], in_sem.at[i])
+
+    def put(i):
+        return pltpu.make_async_copy(slots.at[i], out_ref.at[pl.ds(i * BLOCK, BLOCK)], out_sem.at[i])
+
+    for i in range(3):
+        pl.when(i < length)(lambda: fetch(i).start())
+    for i in (2, 1, 0):
+        @pl.when(i >= length)
+        def _():
+            slots[i] = jnp.zeros(slots.shape[1:], BF16)
+            put(i).start()
+    for i in range(3):
+        @pl.when(i < length)
+        def _():
+            fetch(i).wait()
+            put(i).start()
+    for i in range(3):
+        put(i).wait()
+
+
+def place(mine, offset, n):
+    return pl.pallas_call(
+        functools.partial(placed, n),
+        out_shape=jax.ShapeDtypeStruct(mine.shape, BF16),
+        in_specs=[pl.BlockSpec(memory_space=pltpu.SMEM), pl.BlockSpec(memory_space=pl.ANY)],
+        out_specs=pl.BlockSpec(memory_space=pl.ANY),
+        scratch_shapes=[
+            pltpu.VMEM((3, BLOCK, mine.shape[1]), BF16),
+            pltpu.SemaphoreType.DMA((3,)),
+            pltpu.SemaphoreType.DMA((3,)),
+        ],
+        compiler_params=pltpu.CompilerParams(vmem_limit_bytes=60 * 1024 * 1024),
+    )(offset, mine)
 
 
 def body(n, hn, queries, keys, values, doc_start, decay_rate, gain, plan_offset):
@@ -297,15 +339,19 @@
     heads = width // HD
     hq = heads // GROUP
     vmem = pl.BlockSpec(memory_space=pltpu.VMEM)
+    hbm = pl.BlockSpec(memory_space=pl.ANY)
     smem = pl.BlockSpec(memory_space=pltpu.SMEM)
     dma = pltpu.SemaphoreType.DMA
     partners = max(hn - 1, 1)
-    return pl.pallas_call(
+    mine = pl.pallas_call(
         functools.partial(kernel, n, hn, heads, width),
         out_shape=jax.ShapeDtypeStruct((3 * BLOCK, width), BF16),
-        in_specs=[smem, smem, smem, vmem, vmem, vmem, vmem],
-        out_specs=vmem,
+        in_specs=[smem, smem, vmem, hbm, hbm, hbm],
+        out_specs=hbm,
         scratch_shapes=[
+            pltpu.VMEM((2 * BLOCK, width), BF16),
+            pltpu.VMEM((2 * BLOCK, width), BF16),
+            pltpu.VMEM((2 * BLOCK, width), BF16),
             pltpu.VMEM((2 * BLOCK, width), F32),
             pltpu.VMEM((heads, HD, HD), F32),
             pltpu.VMEM((2, BLOCK, BLOCK), F32),
@@ -319,9 +365,7 @@
             pltpu.VMEM((hq, GROUP, HD, HD), F32),
             pltpu.VMEM((2 * BLOCK, HD), F32),
             pltpu.VMEM((partners, 2 * BLOCK, HD), F32),
-            pltpu.VMEM((BLOCK, width), BF16),
-            pltpu.VMEM((BLOCK, width), BF16),
-            pltpu.VMEM((BLOCK, width), BF16),
+            pltpu.VMEM((2 * BLOCK, width), BF16),
             dma((hq, GROUP - 1)),
             dma((hq, GROUP)),
             dma((hq,)),
@@ -332,11 +376,14 @@
             dma((partners,)),
             dma((CHUNKS,)),
             dma((CHUNKS,)),
+            dma((3,)),
+            dma((2 * CHUNKS,)),
         ],
         compiler_params=pltpu.CompilerParams(
-            collective_id=0, has_side_effects=True, vmem_limit_bytes=48 * 1024 * 1024
+            collective_id=0, has_side_effects=True, vmem_limit_bytes=60 * 1024 * 1024
         ),
-    )(doc_start, decay_rate, plan_offset, queries, keys, values, gain.reshape(1, width))
+    )(doc_start, decay_rate, gain.reshape(1, width), queries, keys, values)
+    return place(mine, plan_offset, n)
 
 
 def solution(mesh):

time: 75.8 us -> 62.3 us (0.82)
  local copies, waits for them, and re-layouts: 9.81 us -> 0 us
  Pallas kernels: 65.1 us -> 62.1 us
    unnamed x13 -> x0, local copies, waits for them, and re-layouts: 9.81 us -> none
    pallas_call x1, Pallas kernels: 65.1 us -> 58.4 us  [body(): pl.pallas_call(functools.partial(kernel, n, hn, heads, width), out_shape=...]
    pallas_call x0 -> x1, Pallas kernels: none -> 3.65 us  [place(): pl.pallas_call(functools.partial(placed, n), out_shape=jax.ShapeDtypeStru...]
where the time goes in v2:
time: 62.3 us; the launch traced here: 62.1 us
  Pallas kernels  62.1 us (100%)
    pallas_call x1, Pallas kernels, body(): pl.pallas_call(functools.partial(kernel, n, hn, heads, width), out_shape=...  58.4 us
    pallas_call x1, Pallas kernels, place(): pl.pallas_call(functools.partial(placed, n), out_shape=jax.ShapeDtypeStru...  3.65 us

profile of v2, /device:TPU:23, one launch (start us, length us, event | category | flops | bytes accessed | tf_op | source)
XLA Modules:
  0.0 62.1 jit_solution(14110666034121147249)
XLA Ops:
  0.0 58.4 %shard_map.73.mine_ref = bf16[768,2048]{1,0:T(8,128)(2,1)} custom-call(s32[2]{0:T(128)} %start_ref.1, f32[16]{0:T(128)} %rate_ref.1, f32[1,2048]{1,0:T(1,128)} %bitcast.1, bf16[512,2048]{1,0:T(8,128)(2,1)} %q_hbm.1, bf16[512,2048]{1,0:T(8,128)(2,1)} %k_hbm.1, bf16[512,2048]{1,0:T(8,128)(2,1)} %v_hbm.1), custom_call_target="tpu_custom_call" | custom-call | tf_op jit(solution)/shard_map/pallas_call | solution.py:346
  58.4 3.7 %shard_map.74 = bf16[768,2048]{1,0:T(8,128)(2,1)} custom-call(s32[16]{0:T(128)} %plan_ref.1, bf16[768,2048]{1,0:T(8,128)(2,1)} %shard_map.73.mine_ref), custom_call_target="tpu_custom_call" | custom-call | tf_op jit(solution)/shard_map/pallas_call | solution.py:323

commit v3 on v2

--- a/solution.py
+++ b/solution.py
@@ -14,6 +14,8 @@
 F32 = jnp.float32
 BF16 = jnp.bfloat16
 CHUNKS = 4
+LEVELS = 32000.0
+TAIL = 16
 CROWS = BLOCK // CHUNKS
 
 
@@ -92,7 +94,22 @@
         u0[h] = parts[0]
         return (flag[1] * power(h, float(BLOCK))) * parts[0] + parts[1]
 
-    both = jnp.full((8, HD), flag[0] * flag[1], F32)
+    both = flag[0] * flag[1]
+
+    def pack(ref, at, tile, bit):
+        largest = jnp.max(jnp.abs(tile), axis=0, keepdims=True)
+        power_of_two = jnp.ceil(jnp.log2(jnp.maximum(largest, 1e-30)))
+        scaled = jnp.round(tile * (LEVELS * jnp.exp2(-power_of_two)))
+        ref[(*at, pl.ds(0, HD))] = scaled.astype(jnp.int32).astype(jnp.int16)
+        code = jnp.broadcast_to(2.0 * power_of_two + bit, (TAIL, HD))
+        ref[(*at, pl.ds(HD, TAIL))] = code.astype(jnp.int32).astype(jnp.int16)
+
+    def unpack(ref, at):
+        code = ref[(*at, pl.ds(HD, TAIL))].astype(jnp.int32)[0:1]
+        bit = (code & 1).astype(F32)
+        power_of_two = (code >> 1).astype(F32)
+        scale = jnp.exp2(power_of_two) * (1.0 / LEVELS)
+        return ref[(*at, pl.ds(0, HD))].astype(jnp.int32).astype(F32) * scale, bit
 
     def p1_copy(c, t):
         to = (r + t) % GROUP
@@ -105,10 +122,8 @@
     def first(c, carry):
         for t in (1, 2, 3):
             to = (r + t) % GROUP
-            sbuf[c, t - 1, 0:HD] = shard_state(to * hq + c)
-            sbuf[c, t - 1, HD:HD + 8] = both
-        p1[c, r, 0:HD] = shard_state(r * hq + c)
-        p1[c, r, HD:HD + 8] = both
+            pack(sbuf, (c, t - 1), shard_state(to * hq + c), both)
+        pack(p1, (c, r), shard_state(r * hq + c), both)
 
         @pl.when(c == 0)
         def _():
@@ -152,8 +167,9 @@
         pre[c, 0, 0:HD] = total
         pre[c, 0, HD:HD + 8] = jnp.ones((8, HD), F32)
         for s in range(GROUP):
-            step = p1[c, s, HD:HD + 1] * decay
-            total = step * total + p1[c, s, 0:HD]
+            part, bit = unpack(p1, (c, s))
+            step = bit * decay
+            total = step * total + part
             reach = reach * step
             pre[c, s + 1, 0:HD] = total
             pre[c, s + 1, HD:HD + 8] = jnp.broadcast_to(reach, (8, HD))
@@ -189,9 +205,9 @@
         incoming = chain_in[c]
         for t in (1, 2, 3):
             to = (r + t) % GROUP
-            p3out[c, t - 1] = pre[c, to, HD:HD + 1] * incoming + pre[c, to, 0:HD]
+            pack(p3out, (c, t - 1), pre[c, to, HD:HD + 1] * incoming + pre[c, to, 0:HD], 0.0)
             p3_copy(c, t).start()
-        p3[c, r] = pre[c, r, HD:HD + 1] * incoming + pre[c, r, 0:HD]
+        pack(p3, (c, r), pre[c, r, HD:HD + 1] * incoming + pre[c, r, 0:HD], 0.0)
         return carry
 
     loads[2].wait()
@@ -205,7 +221,7 @@
             h = src * hq + c
             if t:
                 p3_arrival(c, t).wait_recv()
-            state = p3[c, src]
+            state, _ = unpack(p3, (c, src))
             decay = jnp.exp(-rate_ref[h] * (place_f + 1.0))
             for b in range(2):
                 if b:
@@ -356,13 +372,13 @@
             pltpu.VMEM((heads, HD, HD), F32),
             pltpu.VMEM((2, BLOCK, BLOCK), F32),
             pltpu.VMEM((BLOCK, BLOCK), F32),
-            pltpu.VMEM((hq, GROUP - 1, HD + 8, HD), F32),
-            pltpu.VMEM((hq, GROUP, HD + 8, HD), F32),
+            pltpu.VMEM((hq, GROUP - 1, HD + TAIL, HD), jnp.int16),
+            pltpu.VMEM((hq, GROUP, HD + TAIL, HD), jnp.int16),
             pltpu.VMEM((hq, GROUP + 1, HD + 8, HD), F32),
             pltpu.VMEM((hq, HD, HD), F32),
             pltpu.VMEM((hq, HD, HD), F32),
-            pltpu.VMEM((hq, GROUP - 1, HD, HD), F32),
-            pltpu.VMEM((hq, GROUP, HD, HD), F32),
+            pltpu.VMEM((hq, GROUP - 1, HD + TAIL, HD), jnp.int16),
+            pltpu.VMEM((hq, GROUP, HD + TAIL, HD), jnp.int16),
             pltpu.VMEM((2 * BLOCK, HD), F32),
             pltpu.VMEM((partners, 2 * BLOCK, HD), F32),
             pltpu.VMEM((2 * BLOCK, width), BF16),

time: 62.3 us -> 56.1 us (0.900)
  Pallas kernels: 62.1 us -> 55.9 us
    pallas_call x1, Pallas kernels: 58.4 us -> 52.2 us  [body(): pl.pallas_call(functools.partial(kernel, n, hn, heads, width), out_shape=...]
where the time goes in v3:
time: 56.1 us; the launch traced here: 55.9 us
  Pallas kernels  55.9 us (100%)
    pallas_call x1, Pallas kernels, body(): pl.pallas_call(functools.partial(kernel, n, hn, heads, width), out_shape=...  52.2 us
    pallas_call x1, Pallas kernels, place(): pl.pallas_call(functools.partial(placed, n), out_shape=jax.ShapeDtypeStru...  3.65 us

profile of v3, /device:TPU:23, one launch (start us, length us, event | category | flops | bytes accessed | tf_op | source)
XLA Modules:
  0.0 55.9 jit_solution(16609855621890189716)
XLA Ops:
  0.0 52.2 %shard_map.73.mine_ref = bf16[768,2048]{1,0:T(8,128)(2,1)} custom-call(s32[2]{0:T(128)} %start_ref.1, f32[16]{0:T(128)} %rate_ref.1, f32[1,2048]{1,0:T(1,128)} %bitcast.1, bf16[512,2048]{1,0:T(8,128)(2,1)} %q_hbm.1, bf16[512,2048]{1,0:T(8,128)(2,1)} %k_hbm.1, bf16[512,2048]{1,0:T(8,128)(2,1)} %v_hbm.1), custom_call_target="tpu_custom_call" | custom-call | tf_op jit(solution)/shard_map/pallas_call | solution.py:362
  52.2 3.7 %shard_map.74 = bf16[768,2048]{1,0:T(8,128)(2,1)} custom-call(s32[16]{0:T(128)} %plan_ref.1, bf16[768,2048]{1,0:T(8,128)(2,1)} %shard_map.73.mine_ref), custom_call_target="tpu_custom_call" | custom-call | tf_op jit(solution)/shard_map/pallas_call | solution.py:339
